TPU v7x, 32 devices: a whole 2x2x4 slice. The times are simulated.
32 devices in a mesh: particle: 4 (over y, core), tile: 8 (over z, x).
Axes of the slice: x: 2, y: 2, z: 4, core: 2. Of those that a mesh axis runs over, the one named last changes fastest.
Arguments:
- ensemble: float32 [8, 8, 128, 2048], P('particle', None, 'tile'), may hold values from -6 to 6
- owners: int32 [8], replicated, may hold values from 0 to 7, as said below
- velocity_x: float32 [8, 128, 2048], P(None, 'tile'), may hold values from -0.3 to 0.3
- northward_speed_ratio: float32 [8, 128, 2048], P(None, 'tile'), may hold values from -0.3 to 0.3
- target: float32 [8, 128, 2048], P(None, 'tile'), may hold values from -6 to 6
- forcing: bfloat16 [2, 8, 8, 128, 2048], P(None, 'particle', None, 'tile'), may hold values from -6 to 6
- diffusion: float32 [8], replicated, may hold values from 0.05 to 0.2
- nudging: float32 [8], replicated, may hold values from 0.05 to 0.5
- level_depths: float32 [8], replicated, may hold values from 0.25 to 1
Outputs:
- predicted_ensemble_grids: float32 [8, 8, 2048, 128], P('particle', None, 'tile')
- northward_flux_scaled: float32 [8, 2048, 128], P('particle', 'tile')
Inputs may be any that keep to these rules, and one draw needn't show every extreme that they name: `owners`: 0 and 7 always occur; other members are copied any number of times.
All inputs are finite; a program needn't handle non-finite values.
Results may differ from a plain program's by a relative error of at most 0.0003.
Values sent between devices are 32-bit elements; how exact they have to be, the bound alone decides.
A program may use at most 128 MiB of HBM per device.

v0:
```python
import jax
import jax.numpy as jnp
from jax import lax
from jax.sharding import PartitionSpec as P

forcing_scale = 0.5


def with_halo(value, sides, width):
    for axis, dim in sides:
        size, length = (lax.axis_size(axis), value.shape[dim])
        up = [(i, (i + 1) % size) for i in range(size - 1)]
        down = [(j, i) for i, j in up]
        last = lax.slice_in_dim(value, length - width, length, axis=dim)
        leading = lax.slice_in_dim(value, 0, width, axis=dim)
        before = lax.ppermute(last, axis, up)
        after = lax.ppermute(leading, axis, down)
        value = jnp.concatenate([before, value, after], axis=dim)
    return value


def advance(padded, velocity_x, northward_speed_ratio, diffusion, nudging, target, forcing_now):
    center = padded[..., 1:-1, :]
    northern = padded[..., 2:, :]
    southern = padded[..., :-2, :]
    eastern = jnp.roll(center, -1, axis=-1)
    west_boundary = jnp.roll(center, 1, axis=-1)
    laplace = eastern + west_boundary + northern + southern - 4.0 * center
    advect = 0.5 * velocity_x * (eastern - west_boundary) + 0.5 * northward_speed_ratio * (
        northern - southern
    )
    return (
        center
        - advect
        + diffusion[:, None, None] * laplace
        + nudging[:, None, None] * (target - center)
        + forcing_scale * forcing_now.astype(jnp.float32)
    )


def select(wanted_ids, arrived):
    arrived_count = arrived.shape[0]
    candidates = jnp.arange(arrived_count, dtype=jnp.int32)
    matches = (wanted_ids[:, None] == candidates[None, :]).astype(jnp.float32)
    return jnp.einsum("jk,klrx->jlrx", matches, arrived, precision=lax.Precision.HIGHEST)


def on_device(
    ensemble,
    owners,
    velocity_x,
    northward_speed_ratio,
    target,
    forcing,
    diffusion,
    nudging,
    level_depths,
):
    per_group = ensemble.shape[0]
    member_group = lax.axis_index("particle")
    wanted = lax.dynamic_slice_in_dim(owners, member_group * per_group, per_group)
    prognostic_tracer = select(wanted, lax.all_gather(ensemble, "particle", axis=0, tiled=True))
    steps_total = forcing.shape[0]
    for step_index in range(steps_total):
        padded = with_halo(prognostic_tracer, (("tile", 2),), 1)
        prognostic_tracer = advance(
            padded,
            velocity_x,
            northward_speed_ratio,
            diffusion,
            nudging,
            target,
            forcing[step_index],
        )
    turned = jnp.transpose(prognostic_tracer, (0, 1, 3, 2))
    arrived = lax.all_to_all(turned, "tile", split_axis=2, concat_axis=3, tiled=True)
    vertical_profile = jnp.sum(level_depths[None, :, None, None] * arrived, axis=1)
    northward_flux_scaled = jnp.cumsum(vertical_profile, axis=2) * arrived.shape[3] ** (-0.5)
    return (arrived, northward_flux_scaled)


def solution(mesh):
    placed = (
        P("particle", None, "tile", None),
        P(),
        P(None, "tile", None),
        P(None, "tile", None),
        P(None, "tile", None),
        P(None, "particle", None, "tile", None),
        P(),
        P(),
        P(),
    )
    return jax.shard_map(
        on_device,
        mesh=mesh,
        in_specs=placed,
        out_specs=(P("particle", None, "tile", None), P("particle", "tile", None)),
        check_vma=False,
    )
```

profile of v0, /device:TPU:0, one launch (start us, length us, event | category | flops | bytes accessed | tf_op | source)
XLA Modules:
  0.0 249.0 jit_solution(15386555978910468074)
XLA Ops:
  8.4 1.5 broadcast_multiply_fusion
  10.3 2.6 %convert_multiply_fusion.1 = (f32[1,2,8,16,2048]{4,3,2,1,0:T(8,128)}, f32[1,2,8,16,2048]{4,3,2,1,0:T(8,128)}) fusion(bf16[2,2,8,16,2048]{4,3,2,1,0:T(8,128)(2,1)S(1)} %copy-done.3), kind=kLoop, calls=%fused_computation.8 | loop fusion | flops 2097152 | bytes 6291456 | tf_op jit(solution)/shard_map/mul | solution.py:37
  12.9 57.7 %all-gather.2.cloned.1.call-done = f32[8,8,16,2048]{3,2,1,0:T(8,128)} async-done(((f32[2,8,16,2048]{3,2,1,0:T(8,128)}), f32[8,8,16,2048]{3,2,1,0:T(8,128)}) %all-gather.2.cloned.1.call-update) | async-done | bytes 8388624 | tf_op jit(solution)/shard_map/all_gather | solution.py:62
  70.6 11.9 %fusion = f32[2,8,16,2048]{3,0,2,1:T(2,128)S(1)} fusion(f32[8,8,16,2048]{3,2,1,0:T(8,128)} %all-gather.2.cloned.1.call-done, s32[2]{0:T(128)S(1)} %dynamic_slice.3), kind=kOutput, calls=%fused_computation | convolution fusion | flops 50331664 | bytes 10485768 | tf_op jit(solution)/shard_map/jk,klrx->jlrx/dot_general | solution.py:45
  82.6 2.4 fusion.13
  85.0 3.6 %collective-permute-start.1 = (f32[2,8,1,2048]{3,0,2,1:T(2,128)S(1)}, f32[2,8,1,2048]{3,0,2,1:T(2,128)S(1)}, u32[]{:S(2)}, u32[]{:S(2)}) collective-permute-start(f32[2,8,1,2048]{3,0,2,1:T(2,128)S(1)} %get-tuple-element.24), channel_id=1, source_target_pairs={{0,1},{1,2},{2,3},{3,4},{4,5},{5,6},{6,7},{8,9},{9,10},{10,11},{11... | collective-permute-start | bytes 393224 | tf_op jit(solution)/shard_map/ppermute | solution.py:16
  88.5 1.3 collective-permute-start
  90.0 1.7 collective-permute-done.1
  91.7 4.1 %collective-permute-done = f32[2,8,1,2048]{3,0,2,1:T(2,128)S(1)} collective-permute-done((f32[2,8,1,2048]{3,0,2,1:T(2,128)S(1)}, f32[2,8,1,2048]{3,0,2,1:T(2,128)S(1)}, u32[]{:S(2)}, u32[]{:S(2)}) %collective-permute-start) | collective-permute-done | bytes 131104 | tf_op jit(solution)/shard_map/ppermute | solution.py:17
  95.8 8.0 %fusion.4 = f32[2,8,16,2048]{3,0,2,1:T(2,128)S(1)} fusion(f32[1,2,8,16,2048]{4,3,2,1,0:T(8,128)S(1)} %copy-done.1, f32[2,8,16,2048]{3,0,2,1:T(2,128)S(1)} %fusion, f32[2,8,1,2048]{3,0,2,1:T(2,128)S(1)} %collective-permute-done, f32[2,8,1,2048]{3,0,2,1:T(2,128)S(1)} %collective-permute-done.1, f32[2,8,16,2047]{3,0,2,1:T(2,128)S(1)} %get-tuple-element.21, ...), kind=kLoop, calls=%fused_computation.7 | loop fusion | flops 11010048 | bytes 13893696 | tf_op jit(solution)/shard_map/add | solution.py:33
  103.8 2.4 fusion.10
  106.2 4.3 %collective-permute-start.3 = (f32[2,8,1,2048]{3,0,2,1:T(2,128)S(1)}, f32[2,8,1,2048]{3,0,2,1:T(2,128)S(1)}, u32[]{:S(2)}, u32[]{:S(2)}) collective-permute-start(f32[2,8,1,2048]{3,0,2,1:T(2,128)S(1)} %get-tuple-element.18), channel_id=1, source_target_pairs={{0,1},{1,2},{2,3},{3,4},{4,5},{5,6},{6,7},{8,9},{9,10},{10,11},{11... | collective-permute-start | bytes 393224 | tf_op jit(solution)/shard_map/ppermute | solution.py:16
  110.5 1.3 collective-permute-start.2
  112.0 1.0 collective-permute-done.3
  113.0 4.4 %collective-permute-done.2 = f32[2,8,1,2048]{3,0,2,1:T(2,128)S(1)} collective-permute-done((f32[2,8,1,2048]{3,0,2,1:T(2,128)S(1)}, f32[2,8,1,2048]{3,0,2,1:T(2,128)S(1)}, u32[]{:S(2)}, u32[]{:S(2)}) %collective-permute-start.2) | collective-permute-done | bytes 131104 | tf_op jit(solution)/shard_map/ppermute | solution.py:17
  117.4 8.7 %fusion.3 = f32[2,8,2048,16]{2,0,3,1:T(2,128)} fusion(f32[1,2,8,16,2048]{4,3,2,1,0:T(8,128)S(1)} %copy-done, f32[2,8,16,2048]{3,0,2,1:T(2,128)S(1)} %fusion.4, f32[2,8,1,2048]{3,0,2,1:T(2,128)S(1)} %collective-permute-done.2, f32[2,8,1,2048]{3,0,2,1:T(2,128)S(1)} %collective-permute-done.3, f32[2,8,16,2047]{3,0,2,1:T(2,128)S(1)} %get-tuple-element.15, ...), kind=kLoop, calls=%fused_computation.4 | loop fusion | flops 11010048 | bytes 13893696 | tf_op jit(solution)/shard_map/transpose | solution.py:75
  126.1 11.9 %copy.47 = f32[2,8,2048,16]{3,1,0,2:T(8,128)} copy(f32[2,8,2048,16]{2,0,3,1:T(2,128)} %fusion.3) | data formatting | bytes 4194304 | tf_op jit(solution)/shard_map/transpose | solution.py:75
  138.1 10.6 %reshape.19 = f32[8,1,65536]{2,1,0:T(1,128)S(1)} reshape(f32[2048,2,8,16]{3,2,1,0:T(8,128)} %bitcast.30) | data formatting | bytes 4194304
  148.7 53.2 %all_to_all.18 = f32[8,1,65536]{2,1,0:T(1,128)} all-to-all(f32[8,1,65536]{2,1,0:T(1,128)S(1)} %reshape.19), channel_id=1, replica_groups=mesh['particle'=4,'tile'=8] {'tile'}, dimensions={0} | all-to-all | bytes 4194304 | tf_op jit(solution)/shard_map/all_to_all | solution.py:76
  202.4 7.2 %reduce.1 = f32[8,65536]{1,0:T(8,128)S(1)} reduce(f32[8,1,65536]{2,1,0:T(1,128)} %all_to_all.18, f32[]{:T(128)} %broadcast.31), dimensions={1}, to_apply=%all_to_all.13.reduce_sub_computation | reduce | bytes 4194308 | tf_op jit(solution)/shard_map/all_to_all | solution.py:76
  209.6 11.3 %reshape.20 = f32[2048,2,8,16]{3,2,1,0:T(8,128)} reshape(f32[8,65536]{1,0:T(8,128)S(1)} %reduce.1) | data formatting | bytes 4194304
  220.9 8.3 %copy.54 = f32[2,8,8,256,16]{3,2,4,1,0:T(8,128)S(1)} copy(f32[2,8,8,256,16]{4,1,0,3,2:T(8,128)} %bitcast.28) | data formatting | bytes 4194304 | tf_op jit(solution)/shard_map/all_to_all | solution.py:76
  230.6 9.8 %copy.49 = f32[2,8,256,8,16]{2,4,3,1,0:T(8,128)S(1)} copy(f32[2,8,256,8,16]{4,1,0,2,3:T(8,128)} %bitcast.29) | data formatting | bytes 4194304 | tf_op jit(solution)/shard_map/all_to_all | solution.py:76
  240.4 1.8 copy.51
  (31 shorter events, 4.0 us)
Async XLA Ops:
  7.2 0.8 copy-start.8
  7.2 1.2 copy-start.4
  7.2 63.4 %all-gather.2.cloned.1.call-start = ((), (), s32[]{:S(2)}) async-start(), calls=%async_computation.1 | async-start | bytes 10485760 | tf_op jit(solution)/shard_map/all_gather | solution.py:62
  8.4 1.9 copy-start.3
  82.5 13.3 %copy-start.1 = (f32[1,2,8,16,2048]{4,3,2,1,0:T(8,128)S(1)}, f32[1,2,8,16,2048]{4,3,2,1,0:T(8,128)}, u32[]{:S(2)}) copy-start(f32[1,2,8,16,2048]{4,3,2,1,0:T(8,128)} %get-tuple-element.26) | copy-start | bytes 6291460
  82.5 13.3 %copy-start.2 = (f32[8,16,2048]{2,1,0:T(8,128)S(1)}, f32[8,16,2048]{2,1,0:T(8,128)}, u32[]{:S(2)}) copy-start(f32[8,16,2048]{2,1,0:T(8,128)} %param.13) | copy-start | bytes 3145732
  82.5 13.3 %copy-start.5 = (f32[8]{0:T(128)S(1)}, f32[8]{0:T(128)}, u32[]{:S(2)}) copy-start(f32[8]{0:T(128)} %param.16) | copy-start | bytes 100
  82.5 13.3 %copy-start.6 = (f32[8]{0:T(128)S(1)}, f32[8]{0:T(128)}, u32[]{:S(2)}) copy-start(f32[8]{0:T(128)} %param.15) | copy-start | bytes 100
  85.0 6.7 %collective-permute-start.1 = (f32[2,8,1,2048]{3,0,2,1:T(2,128)S(1)}, f32[2,8,1,2048]{3,0,2,1:T(2,128)S(1)}, u32[]{:S(2)}, u32[]{:S(2)}) collective-permute-start(f32[2,8,1,2048]{3,0,2,1:T(2,128)S(1)} %get-tuple-element.24), channel_id=1, source_target_pairs={{0,1},{1,2},{2,3},{3,4},{4,5},{5,6},{6,7},{8,9},{9,10},{10,11},{11... | collective-permute-start | bytes 393224 | tf_op jit(solution)/shard_map/ppermute | solution.py:16
  88.5 7.3 %collective-permute-start = (f32[2,8,1,2048]{3,0,2,1:T(2,128)S(1)}, f32[2,8,1,2048]{3,0,2,1:T(2,128)S(1)}, u32[]{:S(2)}, u32[]{:S(2)}) collective-permute-start(f32[2,8,1,2048]{3,0,2,1:T(2,128)S(1)} %get-tuple-element.25), channel_id=1, source_target_pairs={{1,0},{2,1},{3,2},{4,3},{5,4},{6,5},{7,6},{9,8},{10,9},{11,10},{12... | collective-permute-start | bytes 393224 | tf_op jit(solution)/shard_map/ppermute | solution.py:17
  103.8 13.6 %copy-start = (f32[1,2,8,16,2048]{4,3,2,1,0:T(8,128)S(1)}, f32[1,2,8,16,2048]{4,3,2,1,0:T(8,128)}, u32[]{:S(2)}) copy-start(f32[1,2,8,16,2048]{4,3,2,1,0:T(8,128)} %get-tuple-element.27) | copy-start | bytes 6291460
  106.2 6.8 %collective-permute-start.3 = (f32[2,8,1,2048]{3,0,2,1:T(2,128)S(1)}, f32[2,8,1,2048]{3,0,2,1:T(2,128)S(1)}, u32[]{:S(2)}, u32[]{:S(2)}) collective-permute-start(f32[2,8,1,2048]{3,0,2,1:T(2,128)S(1)} %get-tuple-element.18), channel_id=1, source_target_pairs={{0,1},{1,2},{2,3},{3,4},{4,5},{5,6},{6,7},{8,9},{9,10},{10,11},{11... | collective-permute-start | bytes 393224 | tf_op jit(solution)/shard_map/ppermute | solution.py:16
  110.5 6.9 %collective-permute-start.2 = (f32[2,8,1,2048]{3,0,2,1:T(2,128)S(1)}, f32[2,8,1,2048]{3,0,2,1:T(2,128)S(1)}, u32[]{:S(2)}, u32[]{:S(2)}) collective-permute-start(f32[2,8,1,2048]{3,0,2,1:T(2,128)S(1)} %get-tuple-element.19), channel_id=1, source_target_pairs={{1,0},{2,1},{3,2},{4,3},{5,4},{6,5},{7,6},{9,8},{10,9},{11,10},{12... | collective-permute-start | bytes 393224 | tf_op jit(solution)/shard_map/ppermute | solution.py:17
  220.9 8.3 %copy-start.7 = (f32[8]{0:T(128)S(1)}, f32[8]{0:T(128)}, u32[]{:S(2)}) copy-start(f32[8]{0:T(128)} %param.17) | copy-start | bytes 100
Sparse Core Ops, SparseCore 0:
  9.6 60.9 all-gather.1
where the time goes:
time: 250 us; the launch traced here: 249 us
  waiting for transfers between devices  69.5 us (28%)
  local copies, waits for them, and re-layouts  61.2 us (24%)
  blocking collectives  53.2 us (21%)
  other arithmetic  28.6 us (11%)
  between operations  14.3 us (6%)
  matrix products  11.9 us (5%)
  starting transfers between devices  10.5 us (4%)
    all_gather x1, waiting for transfers between devices, on_device(): lax.all_gather(ensemble, 'particle', axis=0, tiled=True)  57.7 us
    all_to_all x1, blocking collectives, on_device(): lax.all_to_all(turned, 'tile', split_axis=2, concat_axis=3, tiled=True)  53.2 us
    unnamed x22, local copies, waits for them, and re-layouts  25.3 us
    all_to_all x3, local copies, waits for them, and re-layouts, on_device(): lax.all_to_all(turned, 'tile', split_axis=2, concat_axis=3, tiled=True)  18.6 us
    transpose x1, local copies, waits for them, and re-layouts, on_device(): turned = jnp.transpose(prognostic_tracer, (0, 1, 3, 2))  11.9 us
    dot_general x1, matrix products, select(): jnp.einsum('jk,klrx->jlrx', matches, arrived, precision=lax.Precision.HIG...  11.9 us
    transpose x1, other arithmetic, on_device(): turned = jnp.transpose(prognostic_tracer, (0, 1, 3, 2))  8.74 us
    ppermute x2, waiting for transfers between devices, with_halo(): after = lax.ppermute(leading, axis, down)  8.48 us
  transfers between devices with their start and end apart: 5, of which 5 were waited for; matrix products, arithmetic and copies ran while one was open for 2% of the time, Pallas kernels for 0%

commit v1 on v0

v1 whole, which is shorter than its diff:
```python
import functools

import jax
import jax.numpy as jnp
from jax import lax
from jax.experimental import pallas as pl
from jax.experimental.pallas import tpu as pltpu
from jax.sharding import PartitionSpec as P

forcing_scale = 0.5
MESH = pl.DeviceIdType.MESH


def fused_cycle(
    groups,
    tiles,
    weight_ref,
    diffusion_ref,
    nudging_ref,
    depth_ref,
    ensemble_ref,
    vx_ref,
    vy_ref,
    target_ref,
    forcing_ref,
    out_ref,
    flux_ref,
    chip_members,
    peer_out,
    peer_in,
    vx,
    vy,
    target,
    forcing,
    padded,
    halo_out,
    halo_in,
    blocks_out,
    blocks_in,
    profile,
    own_sem,
    param_sem,
    sibling_send,
    sibling_recv,
    peer_send,
    peer_recv,
    halo_send,
    halo_recv,
    block_send,
    block_recv,
    block_own,
):
    per_group, levels, rows, columns = ensemble_ref.shape
    steps = forcing_ref.shape[0]
    members = groups * per_group
    chips = groups // 2
    width = columns // tiles
    first = 8
    last = first + rows
    me = lax.axis_index("particle")
    tile = lax.axis_index("tile")
    core = lax.rem(me, 2)
    chip = lax.div(me, 2)
    sibling = me + 1 - 2 * core

    def peer(k):
        return lax.rem(me + 2 * k, groups)

    def other_tile(k):
        return lax.rem(tile + k, tiles)

    params = [
        pltpu.make_async_copy(src, dst, param_sem.at[i])
        for i, (src, dst) in enumerate(
            [(vx_ref, vx), (vy_ref, vy), (target_ref, target), (forcing_ref, forcing)]
        )
    ]

    def own_copy(level):
        return pltpu.make_async_copy(
            ensemble_ref.at[:, level], chip_members.at[core, level], own_sem.at[level]
        )

    def sibling_copy(level):
        return pltpu.make_async_remote_copy(
            src_ref=ensemble_ref.at[:, level],
            dst_ref=chip_members.at[core, level],
            send_sem=sibling_send.at[level],
            recv_sem=sibling_recv.at[level],
            device_id=(sibling, tile),
            device_id_type=MESH,
        )

    def sibling_arrival(level):
        return pltpu.make_async_remote_copy(
            src_ref=ensemble_ref.at[:, level],
            dst_ref=chip_members.at[1 - core, level],
            send_sem=sibling_send.at[level],
            recv_sem=sibling_recv.at[level],
            device_id=(sibling, tile),
            device_id_type=MESH,
        )

    def peer_copy(level, k):
        return pltpu.make_async_remote_copy(
            src_ref=peer_out.at[level, k - 1],
            dst_ref=peer_in.at[level, k - 1],
            send_sem=peer_send.at[level, k - 1],
            recv_sem=peer_recv.at[level, k - 1],
            device_id=(peer(k), tile),
            device_id_type=MESH,
        )

    def halo_copy(step, level, side):
        return pltpu.make_async_remote_copy(
            src_ref=halo_out.at[step, level, side],
            dst_ref=halo_in.at[step, level, side],
            send_sem=halo_send.at[step, level, side],
            recv_sem=halo_recv.at[step, level, side],
            device_id=(me, tile + 1 - 2 * side),
            device_id_type=MESH,
        )

    def block_copy(level, k):
        return pltpu.make_async_remote_copy(
            src_ref=blocks_out.at[level, other_tile(k)],
            dst_ref=blocks_in.at[level, tile],
            send_sem=block_send.at[level, k],
            recv_sem=block_recv.at[level, k],
            device_id=(me, other_tile(k)),
            device_id_type=MESH,
        )

    def block_arrival(level, k):
        return pltpu.make_async_remote_copy(
            src_ref=blocks_out.at[level, other_tile(k)],
            dst_ref=blocks_in.at[level, other_tile(tiles - k)],
            send_sem=block_send.at[level, k],
            recv_sem=block_recv.at[level, k],
            device_id=(me, other_tile(k)),
            device_id_type=MESH,
        )

    def block_stay(level):
        return pltpu.make_async_copy(
            blocks_out.at[level, tile], blocks_in.at[level, tile], block_own.at[level]
        )

    def from_chip(level, slot):
        total = None
        for c in range(2):
            for j in range(per_group):
                w = weight_ref[slot * members + chip * (2 * per_group) + c * per_group + j]
                term = w * chip_members[c, level, j]
                total = term if total is None else total + term
        return total

    def send_halo(step, level):
        for j in range(per_group):
            halo_out[step, level, 0, j : j + 1, :] = padded[step, level, j, last - 1 : last, :]
            halo_out[step, level, 1, j : j + 1, :] = padded[step, level, j, first : first + 1, :]

        @pl.when(tile < tiles - 1)
        def _():
            halo_copy(step, level, 0).start()

        @pl.when(tile > 0)
        def _():
            halo_copy(step, level, 1).start()

    def take_halo(step, level):
        zero = jnp.zeros((1, columns), jnp.float32)

        @pl.when(tile > 0)
        def _():
            halo_copy(step, level, 0).wait_recv()
            for j in range(per_group):
                padded[step, level, j, first - 1 : first, :] = halo_in[step, level, 0, j : j + 1, :]

        @pl.when(tile == 0)
        def _():
            for j in range(per_group):
                padded[step, level, j, first - 1 : first, :] = zero

        @pl.when(tile < tiles - 1)
        def _():
            halo_copy(step, level, 1).wait_recv()
            for j in range(per_group):
                padded[step, level, j, last : last + 1, :] = halo_in[step, level, 1, j : j + 1, :]

        @pl.when(tile == tiles - 1)
        def _():
            for j in range(per_group):
                padded[step, level, j, last : last + 1, :] = zero

    def advance(step, level, j):
        d = diffusion_ref[level]
        g = nudging_ref[level]
        hx = 0.5 * vx[level]
        hy = 0.5 * vy[level]
        center = padded[step, level, j, first:last, :]
        north = padded[step, level, j, first + 1 : last + 1, :]
        south = padded[step, level, j, first - 1 : last - 1, :]
        east = pltpu.roll(center, columns - 1, 1)
        west = pltpu.roll(center, 1, 1)
        return (
            (1.0 - 4.0 * d - g) * center
            + (d - hx) * east
            + (d + hx) * west
            + (d - hy) * north
            + (d + hy) * south
            + g * target[level]
            + forcing_scale * forcing[step, j, level].astype(jnp.float32)
        )

    barrier = pltpu.get_barrier_semaphore()
    partners = [(sibling, tile)]
    partners += [(peer(k), tile) for k in range(1, chips)]
    partners += [(me, other_tile(k)) for k in range(1, tiles)]
    for partner in partners:
        pl.semaphore_signal(barrier, inc=1, device_id=partner, device_id_type=MESH)
    for level in range(levels):
        own_copy(level).start()
    for copy in params:
        copy.start()
    pl.semaphore_wait(barrier, len(partners))

    @pl.loop(0, levels)
    def _(level):
        sibling_copy(level).start()

    @pl.loop(0, levels)
    def _(level):
        own_copy(level).wait()
        sibling_arrival(level).wait_recv()
        for k in range(1, chips):
            for j in range(per_group):
                peer_out[level, k - 1, j] = from_chip(level, peer(k) * per_group + j)
            peer_copy(level, k).start()

    for copy in params:
        copy.wait()

    @pl.loop(0, levels + steps)
    def _(turn):
        @pl.when(turn < levels)
        def _():
            level = turn
            for k in range(1, chips):
                peer_copy(level, k).wait_recv()
            for j in range(per_group):
                value = from_chip(level, me * per_group + j)
                for k in range(1, chips):
                    value = value + peer_in[level, k - 1, j]
                padded[0, level, j, first:last, :] = value
            send_halo(0, level)

        for step in range(steps):

            @pl.when((turn >= step + 1) & (turn < levels + step + 1))
            def _():
                level = turn - step - 1
                take_halo(step, level)
                for j in range(per_group):
                    value = advance(step, level, j)
                    if step + 1 < steps:
                        padded[step + 1, level, j, first:last, :] = value
                    else:
                        for t in range(tiles):
                            blocks_out[level, t, j] = value[:, t * width : (t + 1) * width]
                if step + 1 < steps:
                    send_halo(step + 1, level)
                else:
                    block_stay(level).start()
                    for k in range(1, tiles):
                        block_copy(level, k).start()

    profile[...] = jnp.zeros_like(profile)

    @pl.loop(0, levels)
    def _(level):
        block_stay(level).wait()
        for k in range(1, tiles):
            block_arrival(level, k).wait_recv()
        for j in range(per_group):
            whole = blocks_in[level, :, j].reshape(tiles * rows, width)
            turned = whole.T
            out_ref[j, level] = turned
            profile[j] = profile[j] + depth_ref[level] * turned

    extent = tiles * rows
    row = lax.broadcasted_iota(jnp.int32, (extent, extent), 0)
    upto = lax.broadcasted_iota(jnp.int32, (extent, extent), 1)
    mask = (row <= upto).astype(jnp.float32)
    for j in range(per_group):
        flux_ref[j] = jnp.dot(
            profile[j],
            mask,
            precision=lax.Precision.HIGHEST,
            preferred_element_type=jnp.float32,
        ) * extent ** (-0.5)

    @pl.loop(0, levels)
    def _(level):
        sibling_copy(level).wait_send()
        for k in range(1, chips):
            peer_copy(level, k).wait_send()
        for step in range(steps):

            @pl.when(tile < tiles - 1)
            def _():
                halo_copy(step, level, 0).wait_send()

            @pl.when(tile > 0)
            def _():
                halo_copy(step, level, 1).wait_send()

        for k in range(1, tiles):
            block_copy(level, k).wait_send()


def with_kernel(
    groups, tiles, ensemble, owners, velocity_x, velocity_y, target, forcing, diffusion, nudging, depths
):
    per_group, levels, rows, columns = ensemble.shape
    steps = forcing.shape[0]
    members = groups * per_group
    peers = max(groups // 2 - 1, 1)
    width = columns // tiles
    weights = (owners[:, None] == jnp.arange(members, dtype=owners.dtype)[None, :]).astype(jnp.float32)
    f32 = jnp.float32
    dma = pltpu.SemaphoreType.DMA
    smem = pl.BlockSpec(memory_space=pltpu.SMEM)
    anywhere = pl.BlockSpec(memory_space=pl.ANY)
    vmem = pl.BlockSpec(memory_space=pltpu.VMEM)
    points = levels * per_group * rows * columns
    return pl.pallas_call(
        functools.partial(fused_cycle, groups, tiles),
        out_shape=(
            jax.ShapeDtypeStruct((per_group, levels, width, tiles * rows), f32),
            jax.ShapeDtypeStruct((per_group, width, tiles * rows), f32),
        ),
        in_specs=[smem] * 4 + [anywhere] * 5,
        out_specs=(vmem, vmem),
        scratch_shapes=[
            pltpu.VMEM((2, levels, per_group, rows, columns), f32),
            pltpu.VMEM((levels, peers, per_group, rows, columns), f32),
            pltpu.VMEM((levels, peers, per_group, rows, columns), f32),
            pltpu.VMEM(velocity_x.shape, f32),
            pltpu.VMEM(velocity_y.shape, f32),
            pltpu.VMEM(target.shape, f32),
            pltpu.VMEM(forcing.shape, forcing.dtype),
            pltpu.VMEM((steps, levels, per_group, rows + 16, columns), f32),
            pltpu.VMEM((steps, levels, 2, per_group, columns), f32),
            pltpu.VMEM((steps, levels, 2, per_group, columns), f32),
            pltpu.VMEM((levels, tiles, per_group, rows, width), f32),
            pltpu.VMEM((levels, tiles, per_group, rows, width), f32),
            pltpu.VMEM((per_group, width, tiles * rows), f32),
            dma((levels,)),
            dma((4,)),
            dma((levels,)),
            dma((levels,)),
            dma((levels, peers)),
            dma((levels, peers)),
            dma((steps, levels, 2)),
            dma((steps, levels, 2)),
            dma((levels, tiles)),
            dma((levels, tiles)),
            dma((levels,)),
        ],
        compiler_params=pltpu.CompilerParams(
            collective_id=0, has_side_effects=True, vmem_limit_bytes=56 * 1024 * 1024
        ),
        cost_estimate=pl.CostEstimate(
            flops=points * steps * 14, bytes_accessed=points * 20, transcendentals=0
        ),
    )(
        weights.reshape(-1),
        diffusion,
        nudging,
        depths,
        ensemble,
        velocity_x,
        velocity_y,
        target,
        forcing,
    )


def gather_groups(value, axis):
    size = lax.axis_size(axis)
    me = lax.axis_index(axis)
    parts = [value]
    for k in range(1, size):
        parts.append(lax.ppermute(value, axis, [((i + k) % size, i) for i in range(size)]))
    stacked = jnp.concatenate(parts, axis=0)
    return jnp.roll(stacked, me * value.shape[0], axis=0)


def with_halo(value, axis, dim):
    size, length = (lax.axis_size(axis), value.shape[dim])
    up = [(i, (i + 1) % size) for i in range(size - 1)]
    down = [(j, i) for i, j in up]
    before = lax.ppermute(lax.slice_in_dim(value, length - 1, length, axis=dim), axis, up)
    after = lax.ppermute(lax.slice_in_dim(value, 0, 1, axis=dim), axis, down)
    return jnp.concatenate([before, value, after], axis=dim)


def advance_whole(padded, velocity_x, velocity_y, diffusion, nudging, target, forcing_now):
    center = padded[..., 1:-1, :]
    northern = padded[..., 2:, :]
    southern = padded[..., :-2, :]
    eastern = jnp.roll(center, -1, axis=-1)
    western = jnp.roll(center, 1, axis=-1)
    laplace = eastern + western + northern + southern - 4.0 * center
    advect = 0.5 * velocity_x * (eastern - western) + 0.5 * velocity_y * (northern - southern)
    return (
        center
        - advect
        + diffusion[:, None, None] * laplace
        + nudging[:, None, None] * (target - center)
        + forcing_scale * forcing_now.astype(jnp.float32)
    )


def with_collectives(
    ensemble, owners, velocity_x, velocity_y, target, forcing, diffusion, nudging, depths
):
    per_group = ensemble.shape[0]
    wanted = lax.dynamic_slice_in_dim(owners, lax.axis_index("particle") * per_group, per_group)
    gathered = gather_groups(ensemble, "particle")
    candidates = jnp.arange(gathered.shape[0], dtype=owners.dtype)
    matches = (wanted[:, None] == candidates[None, :]).astype(jnp.float32)
    field = jnp.einsum("jk,klrx->jlrx", matches, gathered, precision=lax.Precision.HIGHEST)
    for step in range(forcing.shape[0]):
        padded = with_halo(field, "tile", 2)
        field = advance_whole(
            padded, velocity_x, velocity_y, diffusion, nudging, target, forcing[step]
        )
    turned = jnp.transpose(field, (0, 1, 3, 2))
    arrived = lax.all_to_all(turned, "tile", split_axis=2, concat_axis=3, tiled=True)
    profile = jnp.sum(depths[None, :, None, None] * arrived, axis=1)
    extent = arrived.shape[3]
    upto = jnp.triu(jnp.ones((extent, extent), jnp.float32))
    flux = jnp.einsum("pxr,ry->pxy", profile, upto, precision=lax.Precision.HIGHEST)
    return (arrived, flux * extent ** (-0.5))


def on_device(groups, tiles, ensemble, *others):
    rows, columns = ensemble.shape[2:]
    aligned = columns % (tiles * 128) == 0 and rows % 16 == 0 and (tiles * rows) % 128 == 0
    if aligned and groups % 2 == 0 and groups > 2:
        return with_kernel(groups, tiles, ensemble, *others)
    return with_collectives(ensemble, *others)


def solution(mesh):
    placed = (
        P("particle", None, "tile", None),
        P(),
        P(None, "tile", None),
        P(None, "tile", None),
        P(None, "tile", None),
        P(None, "particle", None, "tile", None),
        P(),
        P(),
        P(),
    )
    return jax.shard_map(
        functools.partial(on_device, mesh.shape["particle"], mesh.shape["tile"]),
        mesh=mesh,
        in_specs=placed,
        out_specs=(P("particle", None, "tile", None), P("particle", "tile", None)),
        check_vma=False,
    )
```

time: 250 us -> 87.9 us (0.35)
  Pallas kernels: 0 us -> 81.9 us
  waiting for transfers between devices: 69.5 us -> 0 us
  local copies, waits for them, and re-layouts: 61.2 us -> 4.45 us
  blocking collectives: 53.2 us -> 0 us
  other arithmetic: 28.6 us -> 0.73 us
  between operations: 14.3 us -> 0.65 us
  matrix products: 11.9 us -> 0 us
  starting transfers between devices: 10.5 us -> 0 us
    pallas_call x0 -> x1, Pallas kernels: none -> 81.9 us  [with_kernel(): pl.pallas_call(functools.partial(fused_cycle, groups, tiles), out_shape=(...]
    all_gather x1 -> x0, waiting for transfers between devices: 57.7 us -> none  [on_device(): lax.all_gather(ensemble, 'particle', axis=0, tiled=True)]
    all_to_all x1 -> x0, blocking collectives: 53.2 us -> none  [on_device(): lax.all_to_all(turned, 'tile', split_axis=2, concat_axis=3, tiled=True)]
    unnamed x22 -> x4, local copies, waits for them, and re-layouts: 25.3 us -> 3.86 us
    all_to_all x3 -> x0, local copies, waits for them, and re-layouts: 18.6 us -> none  [on_device(): lax.all_to_all(turned, 'tile', split_axis=2, concat_axis=3, tiled=True)]
    transpose x1 -> x0, local copies, waits for them, and re-layouts: 11.9 us -> none  [on_device(): turned = jnp.transpose(prognostic_tracer, (0, 1, 3, 2))]
    dot_general x1 -> x0, matrix products: 11.9 us -> none  [select(): jnp.einsum('jk,klrx->jlrx', matches, arrived, precision=lax.Precision.HIG...]
    ppermute x4 -> x0, waiting for transfers between devices: 11.1 us -> none  [the longest x2 8.48 us: with_halo(): after = lax.ppermute(leading, axis, down)]
  transfers between devices with their start and end apart: 5 -> 0, of which waited for: 5 -> 0; matrix products, arithmetic and copies ran while one was open for 2% -> 0% of each run, Pallas kernels for 0% -> 0%
where the time goes in v1:
time: 87.9 us; the launch traced here: 87.7 us
  Pallas kernels  81.9 us (93%)
  local copies, waits for them, and re-layouts  4.45 us (5%)
    pallas_call x1, Pallas kernels, with_kernel(): pl.pallas_call(functools.partial(fused_cycle, groups, tiles), out_shape=(...  81.9 us
    unnamed x4, local copies, waits for them, and re-layouts  3.86 us

profile of v1, /device:TPU:0, one launch (start us, length us, event | category | flops | bytes accessed | tf_op | source)
XLA Modules:
  0.0 87.7 jit_solution(6756094234044060223)
XLA Ops:
  0.6 0.7 fusion
  1.4 0.6 reshape.11.weight_ref
  1.9 81.9 %shard_map.104 = (f32[2,8,256,128]{3,2,1,0:T(8,128)}, f32[2,256,128]{2,1,0:T(8,128)}) custom-call(f32[64]{0:T(128)} %reshape.11.weight_ref, f32[8]{0:T(128)} %diffusion_ref.1, f32[8]{0:T(128)} %nudging_ref.1, f32[8]{0:T(128)} %depth_ref.1, f32[2,8,16,2048]{3,2,1,0:T(8,128)} %ensemble_ref.1, f32[8,16,2048]{2,1,0:T(8,128)} %vx_ref.1, f32[8,16,2048]{2,1,0:T(8,128)} %vy_ref.1, ...), custom_call_target="tpu_custom_call" | custom-call | flops 14680064 | bytes 10485760 | tf_op jit(solution)/shard_map/pallas_call | solution.py:337
  83.8 0.0 copy-start
  83.9 3.2 %copy.13 = f32[2,8,256,128]{3,2,1,0:T(8,128)} copy(f32[2,8,256,128]{3,2,1,0:T(8,128)} %get-tuple-element.4) | data formatting | bytes 4194304
  87.0 0.0 copy-done
  87.0 0.7 copy.14
Async XLA Ops:
  83.8 3.2 %copy-start = (f32[2,256,128]{2,1,0:T(8,128)S(1)}, f32[2,256,128]{2,1,0:T(8,128)}, u32[]{:S(2)}) copy-start(f32[2,256,128]{2,1,0:T(8,128)} %get-tuple-element.5) | copy-start | bytes 786436

commit v2 on v1

--- a/solution.py
+++ b/solution.py
@@ -14,7 +14,7 @@
 def fused_cycle(
     groups,
     tiles,
-    weight_ref,
+    owners_ref,
     diffusion_ref,
     nudging_ref,
     depth_ref,
@@ -37,6 +37,7 @@
     halo_in,
     blocks_out,
     blocks_in,
+    turned,
     profile,
     own_sem,
     param_sem,
@@ -49,14 +50,16 @@
     block_send,
     block_recv,
     block_own,
+    out_sem,
 ):
     per_group, levels, rows, columns = ensemble_ref.shape
     steps = forcing_ref.shape[0]
-    members = groups * per_group
     chips = groups // 2
     width = columns // tiles
     first = 8
     last = first + rows
+    gap = 1
+    pieces = levels * per_group
     me = lax.axis_index("particle")
     tile = lax.axis_index("tile")
     core = lax.rem(me, 2)
@@ -101,106 +104,108 @@
             device_id_type=MESH,
         )
 
-    def peer_copy(level, k):
-        return pltpu.make_async_remote_copy(
-            src_ref=peer_out.at[level, k - 1],
-            dst_ref=peer_in.at[level, k - 1],
-            send_sem=peer_send.at[level, k - 1],
-            recv_sem=peer_recv.at[level, k - 1],
+    def peer_copy(piece, k):
+        return pltpu.make_async_remote_copy(
+            src_ref=peer_out.at[piece, k - 1],
+            dst_ref=peer_in.at[piece, k - 1],
+            send_sem=peer_send.at[piece, k - 1],
+            recv_sem=peer_recv.at[piece, k - 1],
             device_id=(peer(k), tile),
             device_id_type=MESH,
         )
 
-    def halo_copy(step, level, side):
-        return pltpu.make_async_remote_copy(
-            src_ref=halo_out.at[step, level, side],
-            dst_ref=halo_in.at[step, level, side],
-            send_sem=halo_send.at[step, level, side],
-            recv_sem=halo_recv.at[step, level, side],
+    def halo_copy(step, piece, side):
+        return pltpu.make_async_remote_copy(
+            src_ref=halo_out.at[step, piece, side],
+            dst_ref=halo_in.at[step, piece, side],
+            send_sem=halo_send.at[step, piece, side],
+            recv_sem=halo_recv.at[step, piece, side],
             device_id=(me, tile + 1 - 2 * side),
             device_id_type=MESH,
         )
 
-    def block_copy(level, k):
-        return pltpu.make_async_remote_copy(
-            src_ref=blocks_out.at[level, other_tile(k)],
-            dst_ref=blocks_in.at[level, tile],
-            send_sem=block_send.at[level, k],
-            recv_sem=block_recv.at[level, k],
+    def block_copy(piece, k):
+        return pltpu.make_async_remote_copy(
+            src_ref=blocks_out.at[piece, other_tile(k)],
+            dst_ref=blocks_in.at[piece, tile],
+            send_sem=block_send.at[piece, k],
+            recv_sem=block_recv.at[piece, k],
             device_id=(me, other_tile(k)),
             device_id_type=MESH,
         )
 
-    def block_arrival(level, k):
-        return pltpu.make_async_remote_copy(
-            src_ref=blocks_out.at[level, other_tile(k)],
-            dst_ref=blocks_in.at[level, other_tile(tiles - k)],
-            send_sem=block_send.at[level, k],
-            recv_sem=block_recv.at[level, k],
+    def block_arrival(piece, k):
+        return pltpu.make_async_remote_copy(
+            src_ref=blocks_out.at[piece, other_tile(k)],
+            dst_ref=blocks_in.at[piece, other_tile(tiles - k)],
+            send_sem=block_send.at[piece, k],
+            recv_sem=block_recv.at[piece, k],
             device_id=(me, other_tile(k)),
             device_id_type=MESH,
         )
 
-    def block_stay(level):
+    def block_stay(piece):
         return pltpu.make_async_copy(
-            blocks_out.at[level, tile], blocks_in.at[level, tile], block_own.at[level]
-        )
+            blocks_out.at[piece, tile], blocks_in.at[piece, tile], block_own.at[piece]
+        )
+
+    def out_copy(piece):
+        return pltpu.make_async_copy(turned.at[piece], out_ref.at[lax.rem(piece, per_group), lax.div(piece, per_group)], out_sem.at[piece])
 
     def from_chip(level, slot):
+        owner = owners_ref[slot]
         total = None
         for c in range(2):
             for j in range(per_group):
-                w = weight_ref[slot * members + chip * (2 * per_group) + c * per_group + j]
+                member = chip * (2 * per_group) + c * per_group + j
+                w = (owner == member).astype(jnp.float32)
                 term = w * chip_members[c, level, j]
                 total = term if total is None else total + term
         return total
 
-    def send_halo(step, level):
-        for j in range(per_group):
-            halo_out[step, level, 0, j : j + 1, :] = padded[step, level, j, last - 1 : last, :]
-            halo_out[step, level, 1, j : j + 1, :] = padded[step, level, j, first : first + 1, :]
+    def send_halo(step, piece):
+        halo_out[step, piece, 0] = padded[step, piece, last - 1 : last, :]
+        halo_out[step, piece, 1] = padded[step, piece, first : first + 1, :]
 
         @pl.when(tile < tiles - 1)
         def _():
-            halo_copy(step, level, 0).start()
+            halo_copy(step, piece, 0).start()
 
         @pl.when(tile > 0)
         def _():
-            halo_copy(step, level, 1).start()
-
-    def take_halo(step, level):
+            halo_copy(step, piece, 1).start()
+
+    def take_halo(step, piece):
         zero = jnp.zeros((1, columns), jnp.float32)
 
         @pl.when(tile > 0)
         def _():
-            halo_copy(step, level, 0).wait_recv()
-            for j in range(per_group):
-                padded[step, level, j, first - 1 : first, :] = halo_in[step, level, 0, j : j + 1, :]
+            halo_copy(step, piece, 0).wait_recv()
+            padded[step, piece, first - 1 : first, :] = halo_in[step, piece, 0]
 
         @pl.when(tile == 0)
         def _():
-            for j in range(per_group):
-                padded[step, level, j, first - 1 : first, :] = zero
+            padded[step, piece, first - 1 : first, :] = zero
 
         @pl.when(tile < tiles - 1)
         def _():
-            halo_copy(step, level, 1).wait_recv()
-            for j in range(per_group):
-                padded[step, level, j, last : last + 1, :] = halo_in[step, level, 1, j : j + 1, :]
+            halo_copy(step, piece, 1).wait_recv()
+            padded[step, piece, last : last + 1, :] = halo_in[step, piece, 1]
 
         @pl.when(tile == tiles - 1)
         def _():
-            for j in range(per_group):
-                padded[step, level, j, last : last + 1, :] = zero
-
-    def advance(step, level, j):
+            padded[step, piece, last : last + 1, :] = zero
+
+    def advance(step, piece):
+        level = lax.div(piece, per_group)
+        j = lax.rem(piece, per_group)
         d = diffusion_ref[level]
         g = nudging_ref[level]
         hx = 0.5 * vx[level]
         hy = 0.5 * vy[level]
-        center = padded[step, level, j, first:last, :]
-        north = padded[step, level, j, first + 1 : last + 1, :]
-        south = padded[step, level, j, first - 1 : last - 1, :]
+        center = padded[step, piece, first:last, :]
+        north = padded[step, piece, first + 1 : last + 1, :]
+        south = padded[step, piece, first - 1 : last - 1, :]
         east = pltpu.roll(center, columns - 1, 1)
         west = pltpu.roll(center, 1, 1)
         return (
@@ -221,72 +226,73 @@
         pl.semaphore_signal(barrier, inc=1, device_id=partner, device_id_type=MESH)
     for level in range(levels):
         own_copy(level).start()
-    for copy in params:
-        copy.start()
     pl.semaphore_wait(barrier, len(partners))
 
     @pl.loop(0, levels)
     def _(level):
         sibling_copy(level).start()
+
+    for copy in params:
+        copy.start()
 
     @pl.loop(0, levels)
     def _(level):
         own_copy(level).wait()
         sibling_arrival(level).wait_recv()
-        for k in range(1, chips):
-            for j in range(per_group):
-                peer_out[level, k - 1, j] = from_chip(level, peer(k) * per_group + j)
-            peer_copy(level, k).start()
+        for j in range(per_group):
+            for k in range(1, chips):
+                piece = level * per_group + j
+                peer_out[piece, k - 1] = from_chip(level, peer(k) * per_group + j)
+                peer_copy(piece, k).start()
 
     for copy in params:
         copy.wait()
 
-    @pl.loop(0, levels + steps)
+    @pl.loop(0, pieces + gap * steps)
     def _(turn):
-        @pl.when(turn < levels)
-        def _():
-            level = turn
+        @pl.when(turn < pieces)
+        def _():
+            piece = turn
             for k in range(1, chips):
-                peer_copy(level, k).wait_recv()
-            for j in range(per_group):
-                value = from_chip(level, me * per_group + j)
-                for k in range(1, chips):
-                    value = value + peer_in[level, k - 1, j]
-                padded[0, level, j, first:last, :] = value
-            send_halo(0, level)
+                peer_copy(piece, k).wait_recv()
+            value = from_chip(
+                lax.div(piece, per_group), me * per_group + lax.rem(piece, per_group)
+            )
+            for k in range(1, chips):
+                value = value + peer_in[piece, k - 1]
+            padded[0, piece, first:last, :] = value
+            send_halo(0, piece)
 
         for step in range(steps):
 
-            @pl.when((turn >= step + 1) & (turn < levels + step + 1))
+            @pl.when((turn >= gap * (step + 1)) & (turn < pieces + gap * (step + 1)))
             def _():
-                level = turn - step - 1
-                take_halo(step, level)
-                for j in range(per_group):
-                    value = advance(step, level, j)
-                    if step + 1 < steps:
-                        padded[step + 1, level, j, first:last, :] = value
-                    else:
-                        for t in range(tiles):
-                            blocks_out[level, t, j] = value[:, t * width : (t + 1) * width]
+                piece = turn - gap * (step + 1)
+                take_halo(step, piece)
+                value = advance(step, piece)
                 if step + 1 < steps:
-                    send_halo(step + 1, level)
+                    padded[step + 1, piece, first:last, :] = value
+                    send_halo(step + 1, piece)
                 else:
-                    block_stay(level).start()
-                    for k in range(1, tiles):
-                        block_copy(level, k).start()
+                    for t in range(tiles):
+                        blocks_out[piece, t] = value[:, t * width : (t + 1) * width]
+                    block_stay(piece).start()
+                    for k in sorted(range(1, tiles), key=lambda k: abs(k - tiles // 2)):
+                        block_copy(piece, k).start()
 
     profile[...] = jnp.zeros_like(profile)
 
     @pl.loop(0, levels)
     def _(level):
-        block_stay(level).wait()
-        for k in range(1, tiles):
-            block_arrival(level, k).wait_recv()
         for j in range(per_group):
-            whole = blocks_in[level, :, j].reshape(tiles * rows, width)
-            turned = whole.T
-            out_ref[j, level] = turned
-            profile[j] = profile[j] + depth_ref[level] * turned
+            piece = level * per_group + j
+            block_stay(piece).wait()
+            for k in range(1, tiles):
+                block_arrival(piece, k).wait_recv()
+            columns_first = blocks_in[piece].reshape(tiles * rows, width).T
+            turned[piece] = columns_first
+            profile[j] = profile[j] + depth_ref[level] * columns_first
+            out_copy(piece).start()
 
     extent = tiles * rows
     row = lax.broadcasted_iota(jnp.int32, (extent, extent), 0)
@@ -303,20 +309,24 @@
     @pl.loop(0, levels)
     def _(level):
         sibling_copy(level).wait_send()
+
+    @pl.loop(0, pieces)
+    def _(piece):
+        out_copy(piece).wait()
         for k in range(1, chips):
-            peer_copy(level, k).wait_send()
+            peer_copy(piece, k).wait_send()
         for step in range(steps):
 
             @pl.when(tile < tiles - 1)
             def _():
-                halo_copy(step, level, 0).wait_send()
+                halo_copy(step, piece, 0).wait_send()
 
             @pl.when(tile > 0)
             def _():
-                halo_copy(step, level, 1).wait_send()
+                halo_copy(step, piece, 1).wait_send()
 
         for k in range(1, tiles):
-            block_copy(level, k).wait_send()
+            block_copy(piece, k).wait_send()
 
 
 def with_kernel(
@@ -324,15 +334,14 @@
 ):
     per_group, levels, rows, columns = ensemble.shape
     steps = forcing.shape[0]
-    members = groups * per_group
     peers = max(groups // 2 - 1, 1)
     width = columns // tiles
-    weights = (owners[:, None] == jnp.arange(members, dtype=owners.dtype)[None, :]).astype(jnp.float32)
     f32 = jnp.float32
     dma = pltpu.SemaphoreType.DMA
     smem = pl.BlockSpec(memory_space=pltpu.SMEM)
     anywhere = pl.BlockSpec(memory_space=pl.ANY)
     vmem = pl.BlockSpec(memory_space=pltpu.VMEM)
+    pieces = levels * per_group
     points = levels * per_group * rows * columns
     return pl.pallas_call(
         functools.partial(fused_cycle, groups, tiles),
@@ -341,32 +350,34 @@
             jax.ShapeDtypeStruct((per_group, width, tiles * rows), f32),
         ),
         in_specs=[smem] * 4 + [anywhere] * 5,
-        out_specs=(vmem, vmem),
+        out_specs=(anywhere, vmem),
         scratch_shapes=[
             pltpu.VMEM((2, levels, per_group, rows, columns), f32),
-            pltpu.VMEM((levels, peers, per_group, rows, columns), f32),
-            pltpu.VMEM((levels, peers, per_group, rows, columns), f32),
+            pltpu.VMEM((pieces, peers, rows, columns), f32),
+            pltpu.VMEM((pieces, peers, rows, columns), f32),
             pltpu.VMEM(velocity_x.shape, f32),
             pltpu.VMEM(velocity_y.shape, f32),
             pltpu.VMEM(target.shape, f32),
             pltpu.VMEM(forcing.shape, forcing.dtype),
-            pltpu.VMEM((steps, levels, per_group, rows + 16, columns), f32),
-            pltpu.VMEM((steps, levels, 2, per_group, columns), f32),
-            pltpu.VMEM((steps, levels, 2, per_group, columns), f32),
-            pltpu.VMEM((levels, tiles, per_group, rows, width), f32),
-            pltpu.VMEM((levels, tiles, per_group, rows, width), f32),
+            pltpu.VMEM((steps, pieces, rows + 16, columns), f32),
+            pltpu.VMEM((steps, pieces, 2, 1, columns), f32),
+            pltpu.VMEM((steps, pieces, 2, 1, columns), f32),
+            pltpu.VMEM((pieces, tiles, rows, width), f32),
+            pltpu.VMEM((pieces, tiles, rows, width), f32),
+            pltpu.VMEM((pieces, width, tiles * rows), f32),
             pltpu.VMEM((per_group, width, tiles * rows), f32),
             dma((levels,)),
             dma((4,)),
             dma((levels,)),
             dma((levels,)),
-            dma((levels, peers)),
-            dma((levels, peers)),
-            dma((steps, levels, 2)),
-            dma((steps, levels, 2)),
-            dma((levels, tiles)),
-            dma((levels, tiles)),
-            dma((levels,)),
+            dma((pieces, peers)),
+            dma((pieces, peers)),
+            dma((steps, pieces, 2)),
+            dma((steps, pieces, 2)),
+            dma((pieces, tiles)),
+            dma((pieces, tiles)),
+            dma((pieces,)),
+            dma((pieces,)),
         ],
         compiler_params=pltpu.CompilerParams(
             collective_id=0, has_side_effects=True, vmem_limit_bytes=56 * 1024 * 1024
@@ -375,7 +386,7 @@
             flops=points * steps * 14, bytes_accessed=points * 20, transcendentals=0
         ),
     )(
-        weights.reshape(-1),
+        owners,
         diffusion,
         nudging,
         depths,

time: 87.9 us -> 82.8 us (0.942)
  Pallas kernels: 81.9 us -> 78.1 us
    pallas_call x1, Pallas kernels: 81.9 us -> 78.1 us  [with_kernel(): pl.pallas_call(functools.partial(fused_cycle, groups, tiles), out_shape=(...]
where the time goes in v2:
time: 82.8 us; the launch traced here: 82.6 us
  Pallas kernels  78.1 us (94%)
  local copies, waits for them, and re-layouts  3.86 us (5%)
    pallas_call x1, Pallas kernels, with_kernel(): pl.pallas_call(functools.partial(fused_cycle, groups, tiles), out_shape=(...  78.1 us
    unnamed x4, local copies, waits for them, and re-layouts  3.86 us

profile of v2, /device:TPU:0, one launch (start us, length us, event | category | flops | bytes accessed | tf_op | source)
XLA Modules:
  0.0 82.6 jit_solution(7498225704557539868)
XLA Ops:
  0.6 78.1 %shard_map.104 = (f32[2,8,256,128]{3,2,1,0:T(8,128)}, f32[2,256,128]{2,1,0:T(8,128)}) custom-call(s32[8]{0:T(128)} %owners_ref.1, f32[8]{0:T(128)} %diffusion_ref.1, f32[8]{0:T(128)} %nudging_ref.1, f32[8]{0:T(128)} %depth_ref.1, f32[2,8,16,2048]{3,2,1,0:T(8,128)} %ensemble_ref.1, f32[8,16,2048]{2,1,0:T(8,128)} %vx_ref.1, f32[8,16,2048]{2,1,0:T(8,128)} %vy_ref.1, ...), custom_call_target="tpu_custom_call" | custom-call | flops 14680064 | bytes 10485760 | tf_op jit(solution)/shard_map/pallas_call | solution.py:346
  78.7 0.0 copy-start
  78.7 3.2 %copy.13 = f32[2,8,256,128]{3,2,1,0:T(8,128)} copy(f32[2,8,256,128]{3,2,1,0:T(8,128)} %get-tuple-element.4) | data formatting | bytes 4194304
  81.9 0.0 copy-done
  81.9 0.7 copy.14
Async XLA Ops:
  78.7 3.2 %copy-start = (f32[2,256,128]{2,1,0:T(8,128)S(1)}, f32[2,256,128]{2,1,0:T(8,128)}, u32[]{:S(2)}) copy-start(f32[2,256,128]{2,1,0:T(8,128)} %get-tuple-element.5) | copy-start | bytes 786436
